TPU v7x, 256 devices: a whole 4x4x8 slice. The times are simulated.
256 devices in a mesh: ctx: 32 (over z, x), dp: 8 (over y, core).
Axes of the slice: x: 4, y: 4, z: 8, core: 2. Of those that a mesh axis runs over, the one named last changes fastest.
Arguments:
- queries: bfloat16 [8, 8192, 1024], P('dp', 'ctx'), may hold values from -8 to 8
- keys: bfloat16 [8, 8192, 1024], P('dp', 'ctx'), may hold values from -8 to 8
- values: bfloat16 [8, 8192, 1024], P('dp', 'ctx'), may hold values from -6 to 6
- cotangent: bfloat16 [8, 8192, 2048], P('dp', 'ctx'), may hold values from -6 to 6
- proj_weight: bfloat16 [1024, 2048], P('dp'), may hold values from -0.1875 to 0.1875
- pattern: int32 [8, 8, 64, 2], P('dp'), may hold values 0 or 1
Outputs:
- projected: bfloat16 [8, 8192, 2048], P('dp', 'ctx')
- grad_query: bfloat16 [8, 8192, 1024], P('dp', 'ctx')
- grad_key: bfloat16 [8, 8192, 1024], P('dp', 'ctx')
- grad_value: bfloat16 [8, 8192, 1024], P('dp', 'ctx')
- grad_proj: float32 [1024, 2048], P('dp', 'ctx')
Inputs may be any that keep to these rules, and one draw needn't show every extreme that they name: `pattern`: entries with o = 0 or with q - o < 1 are not read.
All inputs are finite; a program needn't handle non-finite values. No bound on the sum of `pattern` on one device may be relied on, other than what follows from the above.
Results may differ from a plain program's by a relative error of at most 0.0085.
The roundings to bfloat16 on the way count: a program that leaves them out, or rounds other values in their place, can miss the bound.
Values may be sent and summed in bfloat16 or wider, within the bound.
A program may use at most 128 MiB of HBM per device.

v0:
```python
import jax
import jax.numpy as jnp
from jax import lax
from jax.sharding import PartitionSpec as P

HEADS = 8
HDIM = 128
BLK = 128
BLK_DEV = 2
WIN = 2
masked_value = -1e30


def shifted(value, axis, steps):
    count = lax.axis_size(axis)
    leading, last = (max(0, -steps), min(count, count - steps))
    return lax.ppermute(value, axis, [(source, source + steps) for source in range(leading, last)])


def spread(block, axis, holder):
    block = jnp.where(lax.axis_index(axis) == holder, block, jnp.zeros_like(block))
    return lax.psum(block, axis)


def product(form, left, right):
    return jnp.einsum(form, left, right, preferred_element_type=jnp.float32)


def block_masks(pattern_rows, query_blocks):
    column = jnp.arange(WIN * BLK, dtype=jnp.int32)
    within = jnp.arange(BLK, dtype=jnp.int32)
    offsets = WIN - 1 - jnp.arange(WIN, dtype=jnp.int32)
    flipped = jnp.flip(pattern_rows, axis=2) == 1
    key_blocks = query_blocks[:, None] - offsets[None, :]
    permitted = (flipped | (offsets == 0)[None, None, :]) & (key_blocks >= 1)[:, None, :]
    expanded = jnp.repeat(permitted, BLK, axis=2)
    causal = (column[None, :] < (WIN - 1) * BLK) | (
        column[None, :] - (WIN - 1) * BLK <= within[:, None]
    )
    key_mask = expanded[:, :, None, :] & causal[None, None, :, :]
    sink_mask = (query_blocks[:, None, None] > 0) | (within[None, None, :] <= within[None, :, None])
    return (key_mask, sink_mask[:, None, :, :])


def attend_scores(queries_b, key_window, sink_keys, key_mask, sink_mask):
    inverse_root = HDIM ** (-0.5)
    scores = product("nqhd,nkhd->nhqk", queries_b, key_window) * inverse_root
    sink_scores = product("nqhd,khd->nhqk", queries_b, sink_keys) * inverse_root
    return (
        jnp.where(key_mask, scores, masked_value),
        jnp.where(sink_mask, sink_scores, masked_value),
    )


def forward_blocks(
    queries_b, key_window, value_window, sink_keys, sink_values, key_mask, sink_mask
):
    scores, sink_scores = attend_scores(queries_b, key_window, sink_keys, key_mask, sink_mask)
    row_max = jnp.maximum(jnp.max(scores, axis=-1), jnp.max(sink_scores, axis=-1))
    row_total = jnp.sum(jnp.exp(scores - row_max[..., None]), axis=-1) + jnp.sum(
        jnp.exp(sink_scores - row_max[..., None]), axis=-1
    )
    log_total = row_max + jnp.log(row_total)
    weights = jnp.exp(scores - log_total[..., None]).astype(jnp.bfloat16)
    sink_weights = jnp.exp(sink_scores - log_total[..., None]).astype(jnp.bfloat16)
    attended = product("nhqk,nkhd->nqhd", weights, value_window) + product(
        "nhqk,khd->nqhd", sink_weights, sink_values
    )
    return (attended.astype(jnp.bfloat16), log_total)


def backward_blocks(
    queries_b,
    key_window,
    value_window,
    sink_keys,
    sink_values,
    key_mask,
    sink_mask,
    log_total,
    out_grad,
    row_delta,
):
    inverse_root = HDIM ** (-0.5)
    scores, sink_scores = attend_scores(queries_b, key_window, sink_keys, key_mask, sink_mask)
    weights = jnp.exp(scores - log_total[..., None])
    sink_weights = jnp.exp(sink_scores - log_total[..., None])
    prob_grad = product("nqhd,nkhd->nhqk", out_grad, value_window)
    sink_prob_grad = product("nqhd,khd->nhqk", out_grad, sink_values)
    score_grad = (weights * (prob_grad - row_delta[..., None])).astype(jnp.bfloat16)
    sink_score_grad = (sink_weights * (sink_prob_grad - row_delta[..., None])).astype(jnp.bfloat16)
    query_grad = inverse_root * (
        product("nhqk,nkhd->nqhd", score_grad, key_window)
        + product("nhqk,khd->nqhd", sink_score_grad, sink_keys)
    )
    window_key_grad = inverse_root * product("nhqk,nqhd->nkhd", score_grad, queries_b)
    window_value_grad = product("nhqk,nqhd->nkhd", weights.astype(jnp.bfloat16), out_grad)
    sink_key_grad = inverse_root * product("nhqk,nqhd->khd", sink_score_grad, queries_b)
    sink_value_grad = product("nhqk,nqhd->khd", sink_weights.astype(jnp.bfloat16), out_grad)
    return (query_grad, window_key_grad, window_value_grad, sink_key_grad, sink_value_grad)


def make_windows(extended, first):
    pieces = [
        extended[(number + first) * BLK : (number + first + WIN) * BLK] for number in range(BLK_DEV)
    ]
    return jnp.stack(pieces).reshape(BLK_DEV, WIN * BLK, HEADS, HDIM)


def place_windows(window_grad):
    flat = window_grad.reshape(BLK_DEV, WIN * BLK, HEADS * HDIM)
    placed = jnp.zeros((2 * BLK_DEV * BLK, HEADS * HDIM), jnp.float32)
    for number in range(BLK_DEV):
        placed = placed + jnp.pad(
            flat[number], (((number + 1) * BLK, (2 * BLK_DEV - number - 1 - WIN) * BLK), (0, 0))
        )
    return placed


def body(queries, keys, values, cotangent, proj_weight, pattern):
    query_rows = queries[0]
    key_rows = keys[0]
    value_rows = values[0]
    grad_output = cotangent[0]
    pattern_doc = pattern[0]
    rows = query_rows.shape[0]
    width_heads = query_rows.shape[1]
    context_index = lax.axis_index("ctx")
    context_count = lax.axis_size("ctx")
    document_count = lax.axis_size("dp")
    prev_keys, prev_values = shifted((key_rows, value_rows), "ctx", 1)
    first_keys, first_values = (
        spread(key_rows[:BLK], "ctx", 0),
        spread(value_rows[:BLK], "ctx", 0),
    )
    full_weight = lax.all_gather(proj_weight, "dp", axis=0, tiled=True)
    query_blocks = context_index * BLK_DEV + jnp.arange(BLK_DEV, dtype=jnp.int32)
    pattern_rows = jnp.transpose(
        lax.dynamic_slice_in_dim(pattern_doc, context_index * BLK_DEV, BLK_DEV, 1), (1, 0, 2)
    )
    key_mask, sink_mask = block_masks(pattern_rows, query_blocks)
    key_window = make_windows(jnp.concatenate([prev_keys, key_rows], axis=0), 1)
    value_window = make_windows(jnp.concatenate([prev_values, value_rows], axis=0), 1)
    query_blocked = query_rows.reshape(BLK_DEV, BLK, HEADS, HDIM)
    sink_keys = first_keys.reshape(BLK, HEADS, HDIM)
    sink_values = first_values.reshape(BLK, HEADS, HDIM)
    attended, log_total = forward_blocks(
        query_blocked, key_window, value_window, sink_keys, sink_values, key_mask, sink_mask
    )
    attended_rows = attended.reshape(rows, width_heads)
    projected = jnp.dot(attended_rows, full_weight, preferred_element_type=jnp.float32).astype(
        jnp.bfloat16
    )
    grad_attended = lax.dot_general(
        grad_output, full_weight, (((1,), (1,)), ((), ())), preferred_element_type=jnp.float32
    ).astype(jnp.bfloat16)
    weight_scale = float(rows * context_count * document_count) ** (-0.5)
    weight_term = (
        lax.dot_general(
            attended_rows, grad_output, (((0,), (0,)), ((), ())), preferred_element_type=jnp.float32
        )
        * weight_scale
    )
    partial_sum = lax.psum_scatter(weight_term, "ctx", scatter_dimension=1, tiled=True)
    grad_proj = lax.psum_scatter(partial_sum, "dp", scatter_dimension=0, tiled=True)
    row_delta = jnp.sum(
        grad_attended.astype(jnp.float32).reshape(rows, HEADS, HDIM)
        * attended_rows.astype(jnp.float32).reshape(rows, HEADS, HDIM),
        axis=-1,
    )
    delta_blocked = jnp.transpose(row_delta.reshape(BLK_DEV, BLK, HEADS), (0, 2, 1))
    grad_blocked = grad_attended.reshape(BLK_DEV, BLK, HEADS, HDIM)
    query_grad, window_key, window_value, sink_key, sink_value = backward_blocks(
        query_blocked,
        key_window,
        value_window,
        sink_keys,
        sink_values,
        key_mask,
        sink_mask,
        log_total,
        grad_blocked,
        delta_blocked,
    )
    sink_key_sum, sink_value_sum = lax.psum((sink_key, sink_value), "ctx")
    placed_keys = place_windows(window_key)
    placed_values = place_windows(window_value)
    later_keys, later_values = shifted((placed_keys[:rows], placed_values[:rows]), "ctx", -1)
    own_key = placed_keys[rows:] + later_keys
    own_value = placed_values[rows:] + later_values
    leading = (context_index == 0).astype(jnp.float32)
    own_key = jnp.concatenate(
        [own_key[:BLK] + leading * sink_key_sum.reshape(BLK, width_heads), own_key[BLK:]], axis=0
    )
    own_value = jnp.concatenate(
        [own_value[:BLK] + leading * sink_value_sum.reshape(BLK, width_heads), own_value[BLK:]],
        axis=0,
    )
    return (
        projected[None],
        query_grad.reshape(rows, width_heads).astype(jnp.bfloat16)[None],
        own_key.astype(jnp.bfloat16)[None],
        own_value.astype(jnp.bfloat16)[None],
        grad_proj,
    )


def solution(mesh):
    return jax.shard_map(
        body,
        mesh=mesh,
        in_specs=(
            P("dp", "ctx", None),
            P("dp", "ctx", None),
            P("dp", "ctx", None),
            P("dp", "ctx", None),
            P("dp", None),
            P("dp", None, None, None),
        ),
        out_specs=(
            P("dp", "ctx", None),
            P("dp", "ctx", None),
            P("dp", "ctx", None),
            P("dp", "ctx", None),
            P("dp", "ctx"),
        ),
        check_vma=False,
    )
```

profile of v0, /device:TPU:2, one launch (start us, length us, event | category | flops | bytes accessed | tf_op | source)
XLA Modules:
  0.0 606.3 jit_solution(17470809247560676850)
XLA Ops:
  8.1 1.3 copy.132
  9.4 1.2 copy.137
  10.7 0.9 copy.143
  11.6 0.9 copy.150
  12.5 0.5 all-gather.2.cloned.1.call-update
  13.1 3.4 collective-permute-start
  16.5 3.1 collective-permute-start.1
  19.6 1.0 copy.135
  20.7 1.2 copy.166
  21.9 1.0 copy.140
  23.6 6.6 %collective-permute-done = bf16[256,1024]{0,1:T(8,128)(2,1)} collective-permute-done((bf16[256,1024]{0,1:T(8,128)(2,1)S(1)}, bf16[256,1024]{0,1:T(8,128)(2,1)}, u32[]{:S(2)}, u32[]{:S(2)}) %collective-permute-start) | collective-permute-done | bytes 524320 | tf_op jit(solution)/shard_map/ppermute | solution.py:17
  30.3 1.0 pad_maximum_fusion.7
  31.3 1.0 copy.134
  32.3 8.6 %collective-permute-done.1 = bf16[256,1024]{0,1:T(8,128)(2,1)} collective-permute-done((bf16[256,1024]{0,1:T(8,128)(2,1)S(1)}, bf16[256,1024]{0,1:T(8,128)(2,1)}, u32[]{:S(2)}, u32[]{:S(2)}) %collective-permute-start.1) | collective-permute-done | bytes 524320 | tf_op jit(solution)/shard_map/ppermute | solution.py:17
  40.9 1.0 pad_maximum_fusion.6
  41.9 1.0 copy.139
  42.9 119.3 %all-reduce.11.cloned.1.call-done = (bf16[128,8,128]{2,0,1:T(8,128)(2,1)}, bf16[128,8,128]{2,0,1:T(8,128)(2,1)}) async-done(((bf16[128,8,128]{2,0,1:T(8,128)(2,1)}, bf16[128,8,128]{2,0,1:T(8,128)(2,1)}), (bf16[128,8,128]{2,0,1:T(8,128)(2,1)}, bf16[128,8,128]{2,0,1:T(8,128)(2,1)})) %all-reduce.11.cloned.1.call-update) | async-done | bytes 524304 | tf_op jit(solution)/shard_map/psum | solution.py:22
  162.2 1.3 fusion.49
  163.5 2.4 fusion.48
  166.4 0.5 copy-done.16
  167.1 0.6 convolution_bitcast_fusion.5
  168.4 0.8 copy-done.13
  169.2 1.3 copy.155
  170.5 3.5 convolution_convert_fusion.1
  174.1 0.9 copy.201
  175.7 0.7 copy.156
  176.4 2.1 copy.174
  178.5 0.8 copy.161
  179.3 2.6 convolution_bitcast_fusion.6
  182.2 0.8 copy-done.14
  183.0 1.1 fusion.13
  184.2 1.4 copy.153
  185.6 0.8 copy-done.20
  186.4 4.6 convolution_multiply_fusion
  191.2 2.1 copy.172
  193.4 2.0 multiply_convert_fusion
  195.4 1.0 copy-done.3
  196.8 0.5 copy-done.15
  197.5 1.1 fusion.10
  198.6 2.1 copy.164
  200.7 2.1 convert_element_type.79
  202.8 1.8 multiply_bitcast_fusion
  204.6 1.5 fusion.47
  206.1 2.6 copy.169
  208.6 2.5 copy.168
  211.2 2.1 pad_add_fusion.1
  213.3 3.6 collective-permute-start.2
  217.6 1.1 pad_add_fusion
  218.7 2.2 collective-permute-start.3
  220.9 2.2 fusion
  223.1 112.2 %all-reduce.9.cloned.1.call-done = (f32[128,8,128]{2,0,1:T(8,128)}, f32[128,8,128]{2,0,1:T(8,128)}) async-done(((f32[128,8,128]{2,0,1:T(8,128)}, f32[128,8,128]{2,0,1:T(8,128)}), (f32[128,8,128]{2,0,1:T(8,128)}, f32[128,8,128]{2,0,1:T(8,128)})) %all-reduce.9.cloned.1.call-update) | async-done | bytes 1048592 | tf_op jit(solution)/shard_map/psum | solution.py:185
  335.4 1.9 broadcast_multiply_fusion.1
  337.2 2.0 copy.171
  339.3 1.4 fusion.15
  340.8 0.9 pad_maximum_fusion.8
  341.7 2.0 copy.178
  343.7 1.9 broadcast_multiply_fusion
  345.6 2.0 copy.177
  347.7 2.4 fusion.17
  350.1 216.8 %reduce-scatter.3.cloned.1.call-done = f32[1024,64]{0,1:T(8,128)} async-done(((f32[1024,2048]{0,1:T(8,128)}), f32[1024,64]{0,1:T(8,128)}) %reduce-scatter.3.cloned.1.call-update) | async-done | bytes 262160 | tf_op jit(solution)/shard_map/reduce_scatter | solution.py:164
  566.9 1.1 fusion.34
  568.0 1.3 fusion.23
  569.3 1.0 copy.179
  570.3 28.9 %reduce-scatter.5.cloned.1.call-done = f32[128,64]{0,1:T(8,128)} async-done(((f32[1024,64]{0,1:T(8,128)}), f32[128,64]{0,1:T(8,128)}) %reduce-scatter.5.cloned.1.call-update) | async-done | bytes 32784 | tf_op jit(solution)/shard_map/reduce_scatter | solution.py:165
  (102 shorter events, 5.2 us)
Async XLA Ops:
  8.0 162.5 %copy-start = (bf16[1,256,2048]{2,1,0:T(8,128)(2,1)S(1)}, bf16[1,256,2048]{2,1,0:T(8,128)(2,1)}, u32[]{:S(2)}) copy-start(bf16[1,256,2048]{2,1,0:T(8,128)(2,1)} %param.9) | copy-start | bytes 3145732
  8.0 154.2 %all-reduce.11.cloned.1.call-start = ((), (), s32[]{:S(2)}) async-start(), calls=%async_computation.6 | async-start | bytes 1048576 | tf_op jit(solution)/shard_map/psum | solution.py:22
  10.6 10.0 %copy-start.27 = (bf16[1,256,1024]{2,1,0:T(8,128)(2,1)S(1)}, bf16[1,256,1024]{2,1,0:T(8,128)(2,1)}, u32[]{:S(2)}) copy-start(bf16[1,256,1024]{2,1,0:T(8,128)(2,1)} %param.6) | copy-start | bytes 1572868
  12.5 158.0 %all-gather.2.cloned.1.call-start = ((), (), s32[]{:S(2)}) async-start(), calls=%async_computation.2 | async-start | bytes 4718592 | tf_op jit(solution)/shard_map/all_gather | solution.py:136
  13.0 322.3 %all-reduce.9.cloned.1.call-start = ((), (), s32[]{:S(2)}) async-start(), calls=%async_computation.5 | async-start | bytes 2097152 | tf_op jit(solution)/shard_map/psum | solution.py:185
  13.1 17.2 %collective-permute-start = (bf16[256,1024]{0,1:T(8,128)(2,1)S(1)}, bf16[256,1024]{0,1:T(8,128)(2,1)}, u32[]{:S(2)}, u32[]{:S(2)}) collective-permute-start(bf16[256,1024]{0,1:T(8,128)(2,1)S(1)} %bitcast.149), channel_id=1, source_target_pairs={{0,8},{8,16},{16,24},{24,32},{32,40},{40,48},{48,56},{56,64},{64,7... | collective-permute-start | bytes 1572872 | tf_op jit(solution)/shard_map/ppermute | solution.py:17
  16.5 24.4 %collective-permute-start.1 = (bf16[256,1024]{0,1:T(8,128)(2,1)S(1)}, bf16[256,1024]{0,1:T(8,128)(2,1)}, u32[]{:S(2)}, u32[]{:S(2)}) collective-permute-start(bf16[256,1024]{0,1:T(8,128)(2,1)S(1)} %bitcast.146), channel_id=1, source_target_pairs={{0,8},{8,16},{16,24},{24,32},{32,40},{40,48},{48,56},{56,64},{64,7... | collective-permute-start | bytes 1572872 | tf_op jit(solution)/shard_map/ppermute | solution.py:17
  19.6 3.3 copy-start.29
  20.7 141.5 %copy-start.10 = (bf16[32,8,8,128]{3,2,1,0:T(8,128)(2,1)}, bf16[32,8,8,128]{3,2,1,0:T(8,128)(2,1)S(1)}, u32[]{:S(2)}) copy-start(bf16[32,8,8,128]{3,2,1,0:T(8,128)(2,1)S(1)} %copy.199) | copy-start | bytes 1572868
  163.5 4.2 copy-start.1
  165.9 1.0 copy-start.16
  165.9 1.2 copy-start.17
  167.1 0.9 copy-start.26
  168.4 0.8 copy-start.13
  173.9 1.4 copy-start.19
  178.5 3.4 copy-start.2
  178.5 3.4 copy-start.18
  179.3 3.7 copy-start.11
  182.2 0.8 copy-start.14
  184.1 382.8 %reduce-scatter.3.cloned.1.call-start = ((), (), s32[]{:S(2)}) async-start(), calls=%async_computation.3 | async-start | bytes 8650752 | tf_op jit(solution)/shard_map/reduce_scatter | solution.py:164
  185.6 0.8 copy-start.20
  191.0 2.4 copy-start.28
  191.0 408.2 %reduce-scatter.5.cloned.1.call-start = ((), (), s32[]{:S(2)}) async-start(), calls=%async_computation.4 | async-start | bytes 294912 | tf_op jit(solution)/shard_map/reduce_scatter | solution.py:165
  193.4 3.0 copy-start.23
  193.4 3.0 copy-start.24
  195.4 1.0 copy-start.3
  196.3 1.0 copy-start.15
  196.3 1.1 copy-start.25
  211.2 5.7 copy-start.12
  213.3 126.0 %collective-permute-start.2 = (f32[256,1024]{0,1:T(8,128)}, f32[256,1024]{0,1:T(8,128)}, u32[]{:S(2)}, u32[]{:S(2)}) collective-permute-start(f32[256,1024]{0,1:T(8,128)} %pad_add_fusion.1), channel_id=1, source_target_pairs={{8,0},{16,8},{24,16},{32,24},{40,32},{48,40},{56,48},{64,56},{72,6... | collective-permute-start | bytes 3145736 | tf_op jit(solution)/shard_map/ppermute | solution.py:17
  217.4 3.5 copy-start.30
  217.6 3.3 copy-start.6
  217.6 3.3 copy-start.8
  217.6 3.3 copy-start.21
  218.7 129.0 %collective-permute-start.3 = (f32[256,1024]{0,1:T(8,128)}, f32[256,1024]{0,1:T(8,128)}, u32[]{:S(2)}, u32[]{:S(2)}) collective-permute-start(f32[256,1024]{0,1:T(8,128)} %pad_add_fusion), channel_id=1, source_target_pairs={{8,0},{16,8},{24,16},{32,24},{40,32},{48,40},{56,48},{64,56},{72,6... | collective-permute-start | bytes 3145736 | tf_op jit(solution)/shard_map/ppermute | solution.py:17
  223.1 116.1 %copy-start.4 = (f32[1,256,8,128]{1,3,2,0:T(8,128)S(1)}, f32[1,256,8,128]{1,3,2,0:T(8,128)}, u32[]{:S(2)}) copy-start(f32[1,256,8,128]{1,3,2,0:T(8,128)} %copy.169) | copy-start | bytes 3145732
  223.1 116.1 %copy-start.5 = (f32[1,256,8,128]{1,3,2,0:T(8,128)S(1)}, f32[1,256,8,128]{1,3,2,0:T(8,128)}, u32[]{:S(2)}) copy-start(f32[1,256,8,128]{1,3,2,0:T(8,128)} %copy.168) | copy-start | bytes 3145732
  339.3 1.5 copy-start.22
  340.8 6.8 %copy-start.7 = (f32[1,256,8,128]{1,3,2,0:T(8,128)S(1)}, f32[1,256,8,128]{1,3,2,0:T(8,128)}, u32[]{:S(2)}) copy-start(f32[1,256,8,128]{1,3,2,0:T(8,128)} %copy-done.6) | copy-start | bytes 3145732
  340.8 6.8 %copy-start.9 = (f32[1,256,8,128]{1,3,2,0:T(8,128)S(1)}, f32[1,256,8,128]{1,3,2,0:T(8,128)}, u32[]{:S(2)}) copy-start(f32[1,256,8,128]{1,3,2,0:T(8,128)} %copy-done.8) | copy-start | bytes 3145732
Sparse Core Ops, SparseCore 0:
  12.9 149.2 all-reduce.10
  184.2 151.0 all-reduce.8
  339.9 226.9 reduce-scatter.2
Sparse Core Ops, SparseCore 1:
  14.8 37.4 all-gather.1
  567.0 32.1 reduce-scatter.4
where the time goes:
time: 608 us; the launch traced here: 606 us
  waiting for transfers between devices  493 us (81%)
  local copies, waits for them, and re-layouts  43.7 us (7%)
  matrix products  24.8 us (4%)
  other arithmetic  16.4 us (3%)
  between operations  15.7 us (3%)
  starting transfers between devices  12.7 us (2%)
    reduce_scatter x1, waiting for transfers between devices, body(): lax.psum_scatter(weight_term, 'ctx', scatter_dimension=1, tiled=True)  217 us
    psum x1, waiting for transfers between devices, spread(): return lax.psum(block, axis)  119 us
    psum x1, waiting for transfers between devices, body(): sink_key_sum, sink_value_sum = lax.psum((sink_key, sink_value), 'ctx')  112 us
    reduce_scatter x1, waiting for transfers between devices, body(): lax.psum_scatter(partial_sum, 'dp', scatter_dimension=0, tiled=True)  28.9 us
    ppermute x4, waiting for transfers between devices, shifted(): lax.ppermute(value, axis, [(source, source + steps) for source in range(l...  15.2 us
    dot_general x12, matrix products, product(): return jnp.einsum(form, left, right, preferred_element_type=jnp.float32)  14.5 us
    ppermute x4, starting transfers between devices, shifted(): lax.ppermute(value, axis, [(source, source + steps) for source in range(l...  12.3 us
  transfers between devices with their start and end apart: 9, of which 6 were waited for; matrix products, arithmetic and copies ran while one was open for 10% of the time, Pallas kernels for 0%

commit v1 on v0

--- a/solution.py
+++ b/solution.py
@@ -19,7 +19,7 @@
 
 def spread(block, axis, holder):
     block = jnp.where(lax.axis_index(axis) == holder, block, jnp.zeros_like(block))
-    return lax.psum(block, axis)
+    return jnp.sum(lax.all_gather(block, axis), axis=0)
 
 
 def product(form, left, right):

time: 608 us -> 689 us (1.13)
  waiting for transfers between devices: 493 us -> 574 us
  other arithmetic: 16.4 us -> 30.1 us
  local copies, waits for them, and re-layouts: 43.7 us -> 33.1 us
    all_gather x0 -> x2, waiting for transfers between devices: none -> 182 us  [spread(): return jnp.sum(lax.all_gather(block, axis), axis=0)]
    psum x1 -> x0, waiting for transfers between devices: 119 us -> none  [spread(): return lax.psum(block, axis)]
    reduce_sum x0 -> x2, other arithmetic: none -> 11.9 us  [spread(): return jnp.sum(lax.all_gather(block, axis), axis=0)]
    psum x1, waiting for transfers between devices: 112 us -> 122 us  [body(): sink_key_sum, sink_value_sum = lax.psum((sink_key, sink_value), 'ctx')]
  transfers between devices with their start and end apart: 9 -> 10, of which waited for: 6 -> 8; matrix products, arithmetic and copies ran while one was open for 10% -> 9% of each run, Pallas kernels for 0% -> 0%
where the time goes in v1:
time: 689 us; the launch traced here: 688 us
  waiting for transfers between devices  574 us (83%)
  local copies, waits for them, and re-layouts  33.1 us (5%)
  other arithmetic  30.1 us (4%)
  matrix products  23.1 us (3%)
  between operations  14.8 us (2%)
  starting transfers between devices  12.7 us (2%)
    reduce_scatter x1, waiting for transfers between devices, body(): lax.psum_scatter(weight_term, 'ctx', scatter_dimension=1, tiled=True)  219 us
    all_gather x2, waiting for transfers between devices, spread(): return jnp.sum(lax.all_gather(block, axis), axis=0)  182 us
    psum x1, waiting for transfers between devices, body(): sink_key_sum, sink_value_sum = lax.psum((sink_key, sink_value), 'ctx')  122 us
    reduce_scatter x1, waiting for transfers between devices, body(): lax.psum_scatter(partial_sum, 'dp', scatter_dimension=0, tiled=True)  33.1 us
  transfers between devices with their start and end apart: 10, of which 8 were waited for; matrix products, arithmetic and copies ran while one was open for 9% of the time, Pallas kernels for 0%

profile of v1, /device:TPU:2, one launch (start us, length us, event | category | flops | bytes accessed | tf_op | source)
XLA Modules:
  0.0 688.2 jit_solution(2636154675789087661)
XLA Ops:
  7.3 0.7 all-gather.8.cloned.1.call-update
  8.0 1.7 slice_select_fusion.1
  9.7 1.7 slice_select_fusion
  11.7 3.4 collective-permute-start
  15.3 3.1 collective-permute-start.1
  18.7 1.0 copy.138
  19.7 1.0 copy.133
  20.7 1.1 copy.201
  21.8 1.1 copy.164
  23.5 5.0 collective-permute-done
  28.5 1.0 pad_maximum_fusion.7
  29.5 1.0 copy.132
  30.5 8.1 %collective-permute-done.1 = bf16[256,1024]{0,1:T(8,128)(2,1)} collective-permute-done((bf16[256,1024]{0,1:T(8,128)(2,1)S(1)}, bf16[256,1024]{0,1:T(8,128)(2,1)}, u32[]{:S(2)}, u32[]{:S(2)}) %collective-permute-start.1) | collective-permute-done | bytes 524320 | tf_op jit(solution)/shard_map/ppermute | solution.py:17
  38.6 1.0 pad_maximum_fusion.6
  39.6 1.0 copy.137
  40.6 2.0 fusion.46
  42.6 5.0 all-gather.8.cloned.1.call-done
  47.6 3.5 convolution_convert_fusion.1
  51.1 0.8 copy-done.23
  51.9 0.9 copy.204
  52.8 2.1 copy.172
  54.9 1.1 convert_bitcast_fusion
  56.1 1.2 copy.205
  57.2 90.0 %all-gather.4.cloned.1.call-done = bf16[32,128,1024]{2,1,0:T(8,128)(2,1)} async-done(((bf16[1,128,1024]{2,1,0:T(8,128)(2,1)}), bf16[32,128,1024]{2,1,0:T(8,128)(2,1)}) %all-gather.4.cloned.1.call-update) | async-done | bytes 8388624 | tf_op jit(solution)/shard_map/all_gather | solution.py:22
  147.2 5.5 reduce_sum.51
  152.8 0.8 copy.202
  153.6 91.7 %all-gather.6.cloned.1.call-done = bf16[32,128,1024]{2,1,0:T(8,128)(2,1)} async-done(((bf16[1,128,1024]{2,1,0:T(8,128)(2,1)}), bf16[32,128,1024]{2,1,0:T(8,128)(2,1)}) %all-gather.6.cloned.1.call-update) | async-done | bytes 8388624 | tf_op jit(solution)/shard_map/all_gather | solution.py:22
  245.3 6.3 reduce_sum.54
  251.6 1.1 copy.146
  252.7 1.5 fusion.47
  254.8 0.9 copy-done.18
  255.6 1.1 convolution_bitcast_fusion.6
  256.8 0.6 convolution_bitcast_fusion.5
  257.8 0.8 copy-done.11
  259.2 0.7 copy.153
  259.9 0.8 copy.159
  260.7 1.8 fusion.9
  262.5 0.8 copy-done.12
  263.3 1.1 fusion.13
  264.7 1.4 copy.150
  266.1 0.8 copy-done.20
  266.8 4.6 convolution_multiply_fusion
  271.5 1.0 copy-done.10
  272.9 1.3 copy.160
  274.9 1.1 pad_add_fusion
  276.2 3.8 collective-permute-start.3
  280.1 0.6 multiply_convert_fusion
  282.4 0.8 copy-done.13
  283.8 1.0 convert_element_type.83
  285.5 1.1 pad_add_fusion.1
  286.6 1.9 collective-permute-start.2
  288.5 4.4 fusion
  293.0 122.1 %all-reduce.7.cloned.1.call-done = (f32[128,8,128]{2,0,1:T(8,128)}, f32[128,8,128]{2,0,1:T(8,128)}) async-done(((f32[128,8,128]{2,0,1:T(8,128)}, f32[128,8,128]{2,0,1:T(8,128)}), (f32[128,8,128]{2,0,1:T(8,128)}, f32[128,8,128]{2,0,1:T(8,128)})) %all-reduce.7.cloned.1.call-update) | async-done | bytes 1048592 | tf_op jit(solution)/shard_map/psum | solution.py:185
  415.1 2.0 broadcast_multiply_fusion
  417.1 2.0 copy.175
  419.1 1.9 broadcast_multiply_fusion.1
  421.0 2.0 copy.169
  423.1 1.7 fusion.17
  425.0 1.0 copy.177
  426.0 1.4 fusion.15
  427.3 218.6 %reduce-scatter.3.cloned.1.call-done = f32[1024,64]{0,1:T(8,128)} async-done(((f32[1024,2048]{0,1:T(8,128)}), f32[1024,64]{0,1:T(8,128)}) %reduce-scatter.3.cloned.1.call-update) | async-done | bytes 262160 | tf_op jit(solution)/shard_map/reduce_scatter | solution.py:164
  646.0 1.2 fusion.24
  647.3 1.0 copy.176
  648.3 33.1 %reduce-scatter.5.cloned.1.call-done = f32[128,64]{0,1:T(8,128)} async-done(((f32[1024,64]{0,1:T(8,128)}), f32[128,64]{0,1:T(8,128)}) %reduce-scatter.5.cloned.1.call-update) | async-done | bytes 32784 | tf_op jit(solution)/shard_map/reduce_scatter | solution.py:165
  (109 shorter events, 7.7 us)
Async XLA Ops:
  7.2 40.4 %copy-start = (bf16[1,256,2048]{2,1,0:T(8,128)(2,1)S(1)}, bf16[1,256,2048]{2,1,0:T(8,128)(2,1)}, u32[]{:S(2)}) copy-start(bf16[1,256,2048]{2,1,0:T(8,128)(2,1)} %param.9) | copy-start | bytes 3145732
  7.2 7.9 %copy-start.28 = (bf16[1,256,1024]{2,1,0:T(8,128)(2,1)S(1)}, bf16[1,256,1024]{2,1,0:T(8,128)(2,1)}, u32[]{:S(2)}) copy-start(bf16[1,256,1024]{2,1,0:T(8,128)(2,1)} %param.7) | copy-start | bytes 1572868
  7.2 4.3 copy-start.27
  7.2 11.3 %copy-start.30 = (s32[1,8,64,2]{2,3,1,0:T(2,128)S(1)}, s32[1,8,64,2]{2,3,1,0:T(2,128)}, u32[]{:S(2)}) copy-start(s32[1,8,64,2]{2,3,1,0:T(2,128)} %param.11) | copy-start | bytes 12292
  7.2 40.4 %all-gather.8.cloned.1.call-start = ((), (), s32[]{:S(2)}) async-start(), calls=%async_computation.4 | async-start | bytes 4718592 | tf_op jit(solution)/shard_map/all_gather | solution.py:136
  7.9 139.3 %all-gather.4.cloned.1.call-start = ((), (), s32[]{:S(2)}) async-start(), calls=%async_computation.2 | async-start | bytes 8650752 | tf_op jit(solution)/shard_map/all_gather | solution.py:22
  9.7 235.6 %all-gather.6.cloned.1.call-start = ((), (), s32[]{:S(2)}) async-start(), calls=%async_computation.3 | async-start | bytes 8650752 | tf_op jit(solution)/shard_map/all_gather | solution.py:22
  11.4 403.7 %all-reduce.7.cloned.1.call-start = ((), (), s32[]{:S(2)}) async-start(), calls=%async_computation.7 | async-start | bytes 2097152 | tf_op jit(solution)/shard_map/psum | solution.py:185
  11.7 16.8 %collective-permute-start = (bf16[256,1024]{0,1:T(8,128)(2,1)S(1)}, bf16[256,1024]{0,1:T(8,128)(2,1)}, u32[]{:S(2)}, u32[]{:S(2)}) collective-permute-start(bf16[256,1024]{0,1:T(8,128)(2,1)S(1)} %bitcast.145), channel_id=1, source_target_pairs={{0,8},{8,16},{16,24},{24,32},{32,40},{40,48},{48,56},{56,64},{64,7... | collective-permute-start | bytes 1572872 | tf_op jit(solution)/shard_map/ppermute | solution.py:17
  15.3 23.3 %collective-permute-start.1 = (bf16[256,1024]{0,1:T(8,128)(2,1)S(1)}, bf16[256,1024]{0,1:T(8,128)(2,1)}, u32[]{:S(2)}, u32[]{:S(2)}) collective-permute-start(bf16[256,1024]{0,1:T(8,128)(2,1)S(1)} %bitcast.142), channel_id=1, source_target_pairs={{0,8},{8,16},{16,24},{24,32},{32,40},{40,48},{48,56},{56,64},{64,7... | collective-permute-start | bytes 1572872 | tf_op jit(solution)/shard_map/ppermute | solution.py:17
  21.8 17.8 %copy-start.8 = (bf16[32,8,8,128]{3,2,1,0:T(8,128)(2,1)}, bf16[32,8,8,128]{3,2,1,0:T(8,128)(2,1)S(1)}, u32[]{:S(2)}) copy-start(bf16[32,8,8,128]{3,2,1,0:T(8,128)(2,1)S(1)} %copy.201) | copy-start | bytes 1572868
  51.1 0.8 copy-start.23
  254.2 3.2 copy-start.2
  254.2 1.4 copy-start.18
  254.6 2.2 copy-start.14
  254.6 2.2 copy-start.16
  257.4 1.5 copy-start.19
  257.8 0.8 copy-start.11
  259.9 3.4 copy-start.9
  262.4 0.8 copy-start.12
  264.4 381.6 %reduce-scatter.3.cloned.1.call-start = ((), (), s32[]{:S(2)}) async-start(), calls=%async_computation.5 | async-start | bytes 8650752 | tf_op jit(solution)/shard_map/reduce_scatter | solution.py:164
  266.1 0.8 copy-start.20
  271.4 1.0 copy-start.10
  271.5 409.9 %reduce-scatter.5.cloned.1.call-start = ((), (), s32[]{:S(2)}) async-start(), calls=%async_computation.6 | async-start | bytes 294912 | tf_op jit(solution)/shard_map/reduce_scatter | solution.py:165
  272.9 1.3 copy-start.6
  274.8 1.4 copy-start.3
  274.8 5.8 copy-start.5
  274.8 5.2 copy-start.7
  274.8 5.2 copy-start.15
  274.9 5.2 copy-start.17
  274.9 5.2 copy-start.29
  276.2 4.5 copy-start.25
  276.2 4.5 copy-start.26
  276.2 146.8 %collective-permute-start.3 = (f32[256,1024]{0,1:T(8,128)}, f32[256,1024]{0,1:T(8,128)}, u32[]{:S(2)}, u32[]{:S(2)}) collective-permute-start(f32[256,1024]{0,1:T(8,128)} %pad_add_fusion), channel_id=1, source_target_pairs={{8,0},{16,8},{24,16},{32,24},{40,32},{48,40},{56,48},{64,56},{72,6... | collective-permute-start | bytes 3145736 | tf_op jit(solution)/shard_map/ppermute | solution.py:17
  280.7 1.0 copy-start.22
  282.2 1.0 copy-start.13
  285.5 3.0 copy-start.21
  286.6 139.4 %collective-permute-start.2 = (f32[256,1024]{0,1:T(8,128)}, f32[256,1024]{0,1:T(8,128)}, u32[]{:S(2)}, u32[]{:S(2)}) collective-permute-start(f32[256,1024]{0,1:T(8,128)} %pad_add_fusion.1), channel_id=1, source_target_pairs={{8,0},{16,8},{24,16},{32,24},{40,32},{48,40},{56,48},{64,56},{72,6... | collective-permute-start | bytes 3145736 | tf_op jit(solution)/shard_map/ppermute | solution.py:17
  415.1 7.9 %copy-start.4 = (f32[1,256,8,128]{1,3,2,0:T(8,128)S(1)}, f32[1,256,8,128]{1,3,2,0:T(8,128)}, u32[]{:S(2)}) copy-start(f32[1,256,8,128]{1,3,2,0:T(8,128)} %copy-done.3) | copy-start | bytes 3145732
  423.0 1.8 copy-start.24
  646.0 35.4 %copy-start.1 = (bf16[1,256,2048]{2,1,0:T(8,128)(2,1)S(1)}, bf16[1,256,2048]{2,1,0:T(8,128)(2,1)}, u32[]{:S(2)}) copy-start(bf16[1,256,2048]{2,1,0:T(8,128)(2,1)} %param.9) | copy-start | bytes 3145732
Sparse Core Ops, SparseCore 0:
  9.9 37.6 all-gather.7
  50.2 97.0 all-gather.3
  149.8 95.4 all-gather.5
  264.5 150.5 all-reduce.6
  419.0 226.9 reduce-scatter.2
  649.1 32.2 reduce-scatter.4
